TPU v7x, 128 devices: a whole 4x4x4 slice. The times are simulated.
128 devices in a mesh: row: 8 (over z, core), col: 16 (over x, y).
Axes of the slice: x: 4, y: 4, z: 4, core: 2. Of those that a mesh axis runs over, the one named last changes fastest.
Arguments:
- loaded: bfloat16 [8192, 4096], P(('row', 'col')), may hold values from -6 to 6
- lengths: int32 [128, 8], replicated, may hold values from 1 to 15, as said below
- offsets: int32 [128, 8], replicated, may hold values from 0 to 8191, as said below
- gate_weight: bfloat16 [4096, 14784], P(None, 'col'), may hold values from -0.09375 to 0.09375
- up_weight: bfloat16 [4096, 14784], P(None, 'col'), may hold values from -0.09375 to 0.09375
- down_weight: bfloat16 [14784, 4096], P('col'), may hold values from -0.046875 to 0.046875
Outputs:
- mixed: bfloat16 [8192, 4096], P('row', 'col')
Inputs may be any that keep to these rules, and one draw needn't show every extreme that they name: Each loader device's pieces 2q and 2q + 1 have lengths summing to 16. `offsets`: every packed position receives exactly one token. The tokens of one loader device that land in one row block of 1024 positions number either 0 or exactly 16; each loader device feeds exactly 4 row blocks.
All inputs are finite; a program needn't handle non-finite values.
Results may differ from a plain program's by a relative error of at most 0.0049.
Values may be sent and summed in bfloat16 or wider, within the bound.
A program may use at most 192 MiB of HBM per device.

v0:
```python
import functools

import jax
import jax.numpy as jnp
from jax import lax
from jax.experimental import pallas as pl
from jax.experimental.pallas import tpu as pltpu
from jax.sharding import PartitionSpec as P

MESH = pl.DeviceIdType.MESH
N_ROW = 8
N_COL = 16
RING = 4
LOAD = 64
CAP = 16
TRAJ = 8
TOK = 1024
HALF = 512
WIDTH = 256
PIECE = 256
SRC = N_ROW * N_COL
NT = (((1,), (1,)), ((), ()))
I32 = jnp.int32
F32 = jnp.float32
BF16 = jnp.bfloat16
GROUPS = ((0,), (4, 12), (1, 3), (8, 2), (5, 7), (13, 15), (6, 14), (9, 11), (10,))
PROGRAM = (
    (0, 1), (1, 1), (0, 0), (0, 3), (2, 0), (1, 0), (3, 4, 1), (0, 2), (4, 0, 0), (2, 1), (3, 1, 0), (3, 12, 0),
    (3, 7, 1), (3, 4, 0), (3, 5, 1), (3, 12, 1), (3, 8, 1), (3, 8, 0), (3, 13, 0), (4, 0, 1), (3, 15, 0),
    (3, 11, 1), (3, 7, 0), (1, 2), (3, 13, 1), (3, 9, 1), (1, 3), (3, 11, 0), (3, 3, 0), (3, 3, 1), (3, 9, 0),
    (3, 1, 1), (4, 0, 2), (3, 15, 1), (3, 5, 0), (4, 0, 7), (2, 3), (2, 2), (4, 0, 4), (4, 0, 5), (3, 6, 1),
    (3, 4, 3), (3, 6, 0), (3, 14, 0), (3, 10, 1), (3, 14, 1), (4, 0, 6), (3, 12, 2), (3, 10, 0), (3, 12, 3),
    (3, 2, 1), (3, 4, 2), (3, 2, 0), (4, 0, 8), (4, 0, 3), (5, 0, 0, 2, 1), (5, 0, 0, 0, 0), (3, 5, 3),
    (3, 1, 2), (3, 1, 3), (5, 0, 0, 1, 1), (4, 1, 1), (5, 0, 0, 2, 0), (3, 8, 3), (3, 8, 2), (3, 3, 2),
    (3, 5, 2), (5, 0, 0, 1, 0), (3, 7, 3), (4, 1, 0), (3, 3, 3), (5, 0, 0, 0, 1), (4, 1, 2), (3, 13, 2),
    (3, 13, 3), (5, 0, 2, 2, 1), (3, 15, 2), (3, 7, 2), (4, 1, 4), (3, 15, 3), (5, 0, 0, 3, 1), (4, 1, 5),
    (3, 11, 3), (5, 0, 0, 3, 0), (3, 6, 3), (3, 11, 2), (5, 0, 1, 2, 0), (3, 2, 2), (5, 0, 1, 2, 1),
    (5, 0, 1, 3, 1), (3, 14, 3), (3, 9, 2), (3, 2, 3), (5, 0, 2, 1, 0), (3, 9, 3), (4, 1, 7), (5, 0, 1, 3, 0),
    (5, 0, 1, 1, 0), (5, 0, 2, 0, 0), (5, 0, 1, 0, 0), (3, 6, 2), (5, 0, 1, 1, 1), (5, 0, 1, 0, 1), (3, 14, 2),
    (5, 0, 2, 3, 1), (5, 0, 2, 3, 0), (4, 1, 6), (5, 0, 2, 1, 1), (3, 10, 2), (5, 0, 3, 0, 1), (4, 1, 3),
    (3, 10, 3), (5, 0, 2, 2, 0), (4, 1, 8), (5, 1, 0, 1, 0), (5, 1, 0, 3, 1), (5, 1, 0, 2, 0), (5, 1, 0, 2, 1),
    (5, 1, 0, 3, 0), (5, 1, 0, 0, 1), (5, 1, 1, 2, 1), (5, 1, 0, 1, 1), (5, 0, 3, 0, 0), (5, 1, 2, 3, 1),
    (5, 0, 4, 0, 0), (5, 1, 2, 1, 0), (5, 1, 0, 0, 0), (5, 1, 1, 3, 1), (5, 1, 1, 0, 0), (5, 1, 1, 2, 0),
    (5, 1, 2, 2, 1), (5, 1, 2, 2, 0), (5, 1, 1, 3, 0), (5, 0, 5, 0, 0), (5, 1, 1, 0, 1), (5, 1, 2, 1, 1),
    (5, 1, 1, 1, 0), (5, 1, 2, 0, 1), (5, 1, 1, 1, 1), (5, 1, 3, 0, 0), (5, 1, 2, 3, 0), (6, 0, 0),
    (5, 1, 3, 0, 1), (5, 0, 4, 0, 1), (5, 0, 5, 0, 1), (5, 1, 2, 0, 0), (5, 0, 2, 0, 1), (5, 1, 4, 0, 0),
    (5, 1, 5, 0, 0), (5, 1, 5, 0, 1), (5, 1, 4, 0, 1), (6, 0, 1), (6, 1, 0), (6, 1, 1),
)


def layer_kernel(
    len_hbm, off_hbm, loaded_hbm, wg_hbm, wu_hbm, wd_hbm, out,
    len_t, off_t, loaded, outgoing, arrived, table, hot, w_in, wd, x, acc, hid, term, got,
    in_sem, w_sem, own_sem, spread_send, spread_recv, ag_send, ag_recv, rs_send, rs_recv,
):
    row = lax.axis_index("row")
    col = lax.axis_index("col")
    me = row * N_COL + col
    cx = lax.div(col, RING)
    cy = lax.rem(col, RING)

    inputs = [
        pltpu.make_async_copy(src, dst, in_sem.at[i])
        for i, (src, dst) in enumerate(
            ((len_hbm, len_t), (off_hbm, off_t), (loaded_hbm, loaded))
        )
    ]
    loads = [
        pltpu.make_async_copy(src, dst, w_sem.at[i])
        for i, (src, dst) in enumerate(((wg_hbm, w_in.at[0]), (wu_hbm, w_in.at[1]), (wd_hbm, wd)))
    ]
    for copy in inputs:
        copy.start()

    def partner(k):
        r = lax.rem(row + lax.div(k, N_COL), N_ROW)
        a = lax.rem(cx + lax.rem(lax.div(k, RING), RING), RING)
        b = lax.rem(cy + lax.rem(k, RING), RING)
        return r, a * RING + b

    barrier = pltpu.get_barrier_semaphore()

    def greet(k, carry):
        pl.semaphore_signal(barrier, inc=1, device_id=partner(k), device_id_type=MESH)
        return carry

    lax.fori_loop(1, SRC, greet, 0)

    for copy in inputs:
        copy.wait()
    for load in loads:
        load.start()
    lane = lax.broadcasted_iota(I32, (LOAD, LOAD), 1)
    sub = lax.broadcasted_iota(I32, (LOAD, LOAD), 0)
    pos_l = jnp.zeros((LOAD, LOAD), I32)
    pos_s = jnp.zeros((LOAD, LOAD), I32)
    own = lax.broadcasted_iota(I32, (TRAJ, SRC), 1) == me
    own_len = jnp.sum(jnp.where(own, len_t[...], 0).astype(F32), axis=1, keepdims=True).astype(I32)
    own_off = jnp.sum(jnp.where(own, off_t[...], 0).astype(F32), axis=1, keepdims=True).astype(I32)
    start = jnp.zeros((1, 1), I32)
    for j in range(TRAJ):
        end = start + own_len[j : j + 1, :]
        shift = own_off[j : j + 1, :] - start
        pos_l = jnp.where((lane >= start) & (lane < end), shift + lane, pos_l)
        pos_s = jnp.where((sub >= start) & (sub < end), shift + sub, pos_s)
        start = end
    block_l = pos_l // TOK
    block_s = pos_s // TOK
    rank = jnp.sum(
        jnp.where((block_l == block_s) & (sub < lane), 1.0, 0.0), axis=0, keepdims=True
    ).astype(I32)
    target = block_l[0:1, :] * CAP + rank
    slot = lax.broadcasted_iota(I32, (N_ROW * CAP, LOAD), 0)
    select = jnp.where(target == slot, 1.0, 0.0).astype(BF16)
    for c in range(N_COL):
        picked = jnp.dot(select, loaded[:, c * WIDTH : (c + 1) * WIDTH], preferred_element_type=F32)
        outgoing[:, c] = picked.astype(BF16).reshape(N_ROW, CAP, WIDTH)
    pl.semaphore_wait(barrier, SRC - 1)

    def spread(k, carry):
        r, c = partner(k)
        pltpu.make_async_remote_copy(
            src_ref=outgoing.at[r, c],
            dst_ref=arrived.at[me],
            send_sem=spread_send,
            recv_sem=spread_recv,
            device_id=(r, c),
            device_id_type=MESH,
        ).start()
        return carry

    lax.fori_loop(1, SRC, spread, 0)
    own_copy = pltpu.make_async_copy(outgoing.at[row, col], arrived.at[me], own_sem)
    own_copy.start()

    tok = lax.broadcasted_iota(I32, (LOAD, SRC), 0)
    pos = jnp.zeros((LOAD, SRC), I32)
    start = jnp.zeros((1, SRC), I32)
    for j in range(TRAJ):
        end = start + len_t[j : j + 1, :]
        pos = jnp.where((tok >= start) & (tok < end), off_t[j : j + 1, :] - start + tok, pos)
        start = end
    mine = pos // TOK == row
    below = jnp.where(sub > lane, 1.0, 0.0).astype(BF16)
    order = jnp.dot(below, jnp.where(mine, 1.0, 0.0).astype(BF16), preferred_element_type=F32)
    order = order.astype(I32)
    in_row = jnp.where(mine, pos % TOK + 1, 0)
    by_slot = jnp.concatenate(
        [
            jnp.sum(jnp.where(order == q, in_row, 0).astype(F32), axis=0, keepdims=True)
            for q in range(CAP)
        ],
        axis=0,
    ).astype(I32)
    wide_s = lax.broadcasted_iota(I32, (SRC, CAP), 0)
    wide_l = lax.broadcasted_iota(I32, (SRC, CAP), 1)
    spread = jnp.where(wide_s % CAP == wide_l, 1.0, 0.0).astype(BF16)
    sq_s = lax.broadcasted_iota(I32, (SRC, SRC), 0)
    sq_l = lax.broadcasted_iota(I32, (SRC, SRC), 1)
    keep = sq_l % 8 == sq_s // CAP
    group_s = lax.broadcasted_iota(I32, (CAP, SRC), 0)
    group_l = lax.broadcasted_iota(I32, (CAP, SRC), 1)
    group = jnp.where(group_l // 8 == group_s, 1.0, 0.0).astype(BF16)
    total = jnp.zeros((CAP, SRC), F32)
    for part, scale in ((by_slot // 32, 32.0), (by_slot % 32, 1.0)):
        y = jnp.dot(spread, part.astype(F32).astype(BF16), preferred_element_type=F32)
        y = jnp.where(keep, y, 0.0).astype(BF16)
        total = total + scale * lax.dot_general(
            group, y, (((1,), (1,)), ((), ())), preferred_element_type=F32
        )
    table[...] = total.astype(I32) - 1

    def place(m, carry):
        first = pl.multiple_of(m * PIECE, PIECE)
        at = lax.broadcasted_iota(I32, (PIECE, SRC), 0) + first
        for g in range(CAP):
            hot[pl.ds(first, PIECE), g * SRC : (g + 1) * SRC] = jnp.where(
                table[g : g + 1, :] == at, 1.0, 0.0
            ).astype(BF16)
        return carry

    lax.fori_loop(0, TOK // PIECE, place, 0)

    swap = lax.rem(row, 2)
    a0 = (1 - swap) * cx + swap * cy
    b0 = (1 - swap) * cy + swap * cx

    def col_of(da, db):
        a = lax.rem(a0 + da, RING)
        b = lax.rem(b0 + db, RING)
        return (1 - swap) * (a * RING + b) + swap * (b * RING + a)

    near = {
        "a+": (row, col_of(1, 0)),
        "a-": (row, col_of(3, 0)),
        "b+": (row, col_of(0, 1)),
        "b-": (row, col_of(0, 3)),
    }
    own_copy.wait()
    others = arrived.at[pl.ds(0, SRC - 1)]
    pltpu.make_async_copy(others, others, spread_recv).wait()

    def compact(m):
        def one(i, carry):
            part = pl.ds(pl.multiple_of(i * 128, 128), 128)
            from_row = pl.ds(pl.multiple_of(m * PIECE + i * 128, 128), 128)
            x[0, m, part, :] = jnp.dot(
                hot[from_row, :],
                arrived[...].reshape(SRC * CAP, WIDTH),
                preferred_element_type=F32,
            ).astype(BF16)
            return carry

        lax.fori_loop(0, PIECE // 128, one, 0)

    sends = {}
    count = [0]

    def forward(slot, m, way, to):
        copy = pltpu.make_async_remote_copy(
            src_ref=x.at[slot, m],
            dst_ref=x.at[to, m],
            send_sem=ag_send.at[count[0]],
            recv_sem=ag_recv.at[to, m],
            device_id=near[way],
            device_id_type=MESH,
        )
        count[0] += 1
        copy.start()
        sends.setdefault((slot, m), []).append(copy)

    def own_first(m):
        forward(0, m, "a-", 1 * RING)
        forward(0, m, "a+", 3 * RING)

    def own_second(m):
        forward(0, m, "b-", 1)
        forward(0, m, "b+", 3)

    def take(slot, m):
        pltpu.make_async_copy(x.at[slot, m], x.at[slot, m], ag_recv.at[slot, m]).wait()
        da, db, q = slot // RING, slot % RING, m % 2
        if db == 0:
            if da == 3 and q == 0:
                forward(slot, m, "a+", 2 * RING)
            if da == 1 and q == 1:
                forward(slot, m, "a-", 2 * RING)
            forward(slot, m, "b-", da * RING + 1)
            forward(slot, m, "b+", da * RING + 3)
        if db == 3 and q == 0:
            forward(slot, m, "b+", da * RING + 2)
        if db == 1 and q == 1:
            forward(slot, m, "b-", da * RING + 2)

    done = [0, 0]

    def gate_up(t, group):
        if sum(done) == 0:
            for load in loads[:2]:
                load.wait()
        slots = GROUPS[group]
        first, last = done[t] == 0, done[t] == len(GROUPS) - 1
        done[t] += 1
        ks = [
            pl.ds(pl.multiple_of(col_of(s // RING, s % RING) * WIDTH, WIDTH), WIDTH) for s in slots
        ]

        def one(which, carry):
            value = None
            for s, k in zip(slots, ks):
                lhs = x[s, 2 * t : 2 * t + 2].reshape(HALF, WIDTH)
                part = lax.dot_general(lhs, w_in[which, :, k], NT, preferred_element_type=F32)
                value = part if value is None else value + part
            acc[which] = value if first else acc[which] + value
            return carry

        lax.fori_loop(0, 2, one, 0)
        if last:

            def activate(i, carry):
                part = pl.ds(pl.multiple_of(i * 128, 128), 128)
                g = acc[0, part, :]
                u = acc[1, part, :]
                to = pl.ds(pl.multiple_of(t * HALF + i * 128, 128), 128)
                hid[to, :] = (g / (1.0 + jnp.exp(-g)) * u).astype(BF16)
                return carry

            lax.fori_loop(0, HALF // 128, activate, 0)

    order = [2, 6, 14, 10, 0, 1, 3, 4, 12, 5, 7, 13, 15, 8, 9, 11]
    spots = [[(s, 2 * t + q) for s in order for q in (0, 1)] for t in (0, 1)]
    started = []

    def product(slot, m):
        cols = pl.ds(pl.multiple_of(col_of(slot // RING, slot % RING) * WIDTH, WIDTH), WIDTH)

        def one(i, carry):
            part = pl.ds(pl.multiple_of(i * 128, 128), 128)
            from_row = pl.ds(pl.multiple_of(m * PIECE + i * 128, 128), 128)
            term[part, :] = jnp.dot(hid[from_row, :], wd[:, cols], preferred_element_type=F32)
            return carry

        lax.fori_loop(0, PIECE // 128, one, 0)
        return term[...]

    def landed(i, t):
        i = t * 30 + i
        pltpu.make_async_copy(got.at[i], got.at[i], rs_recv.at[i]).wait()
        return got[i].astype(F32)

    def send(value, way, to, t):
        n = len(started)
        spot = spots[t].pop(0)
        for copy in sends.pop(spot, []):
            copy.wait_send()
        x[spot[0], spot[1]] = value.astype(BF16)
        to = t * 30 + to
        copy = pltpu.make_async_remote_copy(
            src_ref=x.at[spot[0], spot[1]],
            dst_ref=got.at[to],
            send_sem=rs_send.at[n],
            recv_sem=rs_recv.at[to],
            device_id=near[way],
            device_id_type=MESH,
        )
        copy.start()
        started.append(copy)

    def chain(da, q):
        return da * 2 + q

    def plus(da, q):
        return 8 + da * 2 + q

    def minus(da, q):
        return 16 + da * 2 + q

    def scatter(t, kind, da, q):
        if kind == 0:
            send(product(da * RING + 2, 2 * t + q), "b+" if q else "b-", chain(da, q), t)
        elif kind == 1:
            if q:
                send(product(da * RING + 3, 2 * t + 1), "b-", plus(da, 1), t)
            else:
                send(product(da * RING + 1, 2 * t), "b+", minus(da, 0), t)
        elif kind == 2:
            if q:
                value = product(da * RING + 1, 2 * t + 1) + landed(chain(da, 1), t)
                send(value, "b+", minus(da, 1), t)
            else:
                value = product(da * RING + 3, 2 * t) + landed(chain(da, 0), t)
                send(value, "b-", plus(da, 0), t)
        elif kind == 3:
            send(total(t, 2, q), "a+" if q else "a-", 24 + q, t)
        elif kind == 4:
            if q:
                send(total(t, 3, 1), "a-", 27, t)
            else:
                send(total(t, 1, 0), "a+", 28, t)
        elif q:
            send(total(t, 1, 1) + landed(25, t), "a+", 29, t)
        else:
            send(total(t, 3, 0) + landed(24, t), "a-", 26, t)

    def total(t, da, q):
        return product(da * RING, 2 * t + q) + landed(plus(da, q), t) + landed(minus(da, q), t)

    def finish(t, q):
        m = 2 * t + q
        value = total(t, 0, q) + landed(26 + q, t) + landed(28 + q, t)
        out[m * PIECE : (m + 1) * PIECE, :] = value.astype(BF16)

    steps = (compact, own_first, own_second, take, gate_up, scatter, finish)
    for what, *which in PROGRAM:
        if what == 5 and not started:
            loads[2].wait()
        steps[what](*which)
    for copies in sends.values():
        for copy in copies:
            copy.wait_send()
    for copy in started:
        copy.wait_send()
    pltpu.make_async_copy(others, others, spread_send).wait()


def per_device(loaded, lengths, offsets, gate_weight, up_weight, down_weight):
    width, hidden = gate_weight.shape
    hbm = pl.BlockSpec(memory_space=pl.ANY)
    return pl.pallas_call(
        layer_kernel,
        out_shape=jax.ShapeDtypeStruct((TOK, WIDTH), BF16),
        in_specs=[hbm] * 6,
        out_specs=pl.BlockSpec(memory_space=pltpu.VMEM),
        scratch_shapes=[
            pltpu.VMEM((TRAJ, SRC), I32),
            pltpu.VMEM((TRAJ, SRC), I32),
            pltpu.VMEM((LOAD, width), BF16),
            pltpu.VMEM((N_ROW, N_COL, CAP, WIDTH), BF16),
            pltpu.VMEM((SRC, CAP, WIDTH), BF16),
            pltpu.VMEM((CAP, SRC), I32),
            pltpu.VMEM((TOK, SRC * CAP), BF16),
            pltpu.VMEM((2, hidden, width), BF16),
            pltpu.VMEM((hidden, width), BF16),
            pltpu.VMEM((N_COL, 4, PIECE, WIDTH), BF16),
            pltpu.VMEM((2, HALF, hidden), F32),
            pltpu.VMEM((TOK, hidden), BF16),
            pltpu.VMEM((PIECE, WIDTH), F32),
            pltpu.VMEM((60, PIECE, WIDTH), BF16),
            pltpu.SemaphoreType.DMA((3,)),
            pltpu.SemaphoreType.DMA((3,)),
            pltpu.SemaphoreType.DMA,
            pltpu.SemaphoreType.DMA,
            pltpu.SemaphoreType.DMA,
            pltpu.SemaphoreType.DMA((60,)),
            pltpu.SemaphoreType.DMA((N_COL, 4)),
            pltpu.SemaphoreType.DMA((60,)),
            pltpu.SemaphoreType.DMA((60,)),
        ],
        compiler_params=pltpu.CompilerParams(
            collective_id=0, has_side_effects=True, vmem_limit_bytes=60 * 1024 * 1024
        ),
        name="layer",
    )(lengths.T, offsets.T, loaded, gate_weight.T, up_weight.T, down_weight)


def solution(mesh):
    placed = (P(("row", "col"), None), P(), P(), P(None, "col"), P(None, "col"), P("col", None))
    return jax.shard_map(
        per_device, mesh=mesh, in_specs=placed, out_specs=P("row", "col"), check_vma=False
    )
```

profile of v0, /device:TPU:1, one launch (start us, length us, event | category | flops | bytes accessed | tf_op | source)
XLA Modules:
  0.0 124.3 jit_solution(4023508440473695727)
XLA Ops:
  0.0 122.5 %layer.1 = bf16[1024,256]{1,0:T(8,128)(2,1)} custom-call(s32[8,128]{1,0:T(8,128)} %bitcast.6, s32[8,128]{1,0:T(8,128)} %bitcast.7, bf16[64,4096]{1,0:T(8,128)(2,1)} %loaded_hbm.1, bf16[924,4096]{1,0:T(8,128)(2,1)} %bitcast.4, bf16[924,4096]{1,0:T(8,128)(2,1)} %bitcast.5, bf16[924,4096]{1,0:T(8,128)(2,1)} %wd_hbm.1), custom_call_target="tpu_custom_call" | custom-call | tf_op jit(solution)/shard_map/layer/pallas_call | solution.py:389
  122.5 1.9 %copy.8 = bf16[1024,256]{1,0:T(8,128)(2,1)} copy(bf16[1024,256]{1,0:T(8,128)(2,1)} %layer.1) | data formatting | bytes 1048576
where the time goes:
time: 126 us; the launch traced here: 124 us
  Pallas kernels  122 us (97%)
  local copies, waits for them, and re-layouts  1.87 us (1%)
    pallas_call x1, Pallas kernels, per_device(): pl.pallas_call(layer_kernel, out_shape=jax.ShapeDtypeStruct((TOK, WIDTH),...  122 us

commit v1 on v0

--- a/solution.py
+++ b/solution.py
@@ -18,6 +18,7 @@
 HALF = 512
 WIDTH = 256
 PIECE = 256
+STRIDE = 85
 SRC = N_ROW * N_COL
 NT = (((1,), (1,)), ((), ()))
 I32 = jnp.int32
@@ -25,26 +26,26 @@
 BF16 = jnp.bfloat16
 GROUPS = ((0,), (4, 12), (1, 3), (8, 2), (5, 7), (13, 15), (6, 14), (9, 11), (10,))
 PROGRAM = (
-    (0, 1), (1, 1), (0, 0), (0, 3), (2, 0), (1, 0), (3, 4, 1), (0, 2), (4, 0, 0), (2, 1), (3, 1, 0), (3, 12, 0),
-    (3, 7, 1), (3, 4, 0), (3, 5, 1), (3, 12, 1), (3, 8, 1), (3, 8, 0), (3, 13, 0), (4, 0, 1), (3, 15, 0),
-    (3, 11, 1), (3, 7, 0), (1, 2), (3, 13, 1), (3, 9, 1), (1, 3), (3, 11, 0), (3, 3, 0), (3, 3, 1), (3, 9, 0),
-    (3, 1, 1), (4, 0, 2), (3, 15, 1), (3, 5, 0), (4, 0, 7), (2, 3), (2, 2), (4, 0, 4), (4, 0, 5), (3, 6, 1),
-    (3, 4, 3), (3, 6, 0), (3, 14, 0), (3, 10, 1), (3, 14, 1), (4, 0, 6), (3, 12, 2), (3, 10, 0), (3, 12, 3),
-    (3, 2, 1), (3, 4, 2), (3, 2, 0), (4, 0, 8), (4, 0, 3), (5, 0, 0, 2, 1), (5, 0, 0, 0, 0), (3, 5, 3),
-    (3, 1, 2), (3, 1, 3), (5, 0, 0, 1, 1), (4, 1, 1), (5, 0, 0, 2, 0), (3, 8, 3), (3, 8, 2), (3, 3, 2),
-    (3, 5, 2), (5, 0, 0, 1, 0), (3, 7, 3), (4, 1, 0), (3, 3, 3), (5, 0, 0, 0, 1), (4, 1, 2), (3, 13, 2),
-    (3, 13, 3), (5, 0, 2, 2, 1), (3, 15, 2), (3, 7, 2), (4, 1, 4), (3, 15, 3), (5, 0, 0, 3, 1), (4, 1, 5),
-    (3, 11, 3), (5, 0, 0, 3, 0), (3, 6, 3), (3, 11, 2), (5, 0, 1, 2, 0), (3, 2, 2), (5, 0, 1, 2, 1),
-    (5, 0, 1, 3, 1), (3, 14, 3), (3, 9, 2), (3, 2, 3), (5, 0, 2, 1, 0), (3, 9, 3), (4, 1, 7), (5, 0, 1, 3, 0),
-    (5, 0, 1, 1, 0), (5, 0, 2, 0, 0), (5, 0, 1, 0, 0), (3, 6, 2), (5, 0, 1, 1, 1), (5, 0, 1, 0, 1), (3, 14, 2),
-    (5, 0, 2, 3, 1), (5, 0, 2, 3, 0), (4, 1, 6), (5, 0, 2, 1, 1), (3, 10, 2), (5, 0, 3, 0, 1), (4, 1, 3),
-    (3, 10, 3), (5, 0, 2, 2, 0), (4, 1, 8), (5, 1, 0, 1, 0), (5, 1, 0, 3, 1), (5, 1, 0, 2, 0), (5, 1, 0, 2, 1),
-    (5, 1, 0, 3, 0), (5, 1, 0, 0, 1), (5, 1, 1, 2, 1), (5, 1, 0, 1, 1), (5, 0, 3, 0, 0), (5, 1, 2, 3, 1),
-    (5, 0, 4, 0, 0), (5, 1, 2, 1, 0), (5, 1, 0, 0, 0), (5, 1, 1, 3, 1), (5, 1, 1, 0, 0), (5, 1, 1, 2, 0),
-    (5, 1, 2, 2, 1), (5, 1, 2, 2, 0), (5, 1, 1, 3, 0), (5, 0, 5, 0, 0), (5, 1, 1, 0, 1), (5, 1, 2, 1, 1),
-    (5, 1, 1, 1, 0), (5, 1, 2, 0, 1), (5, 1, 1, 1, 1), (5, 1, 3, 0, 0), (5, 1, 2, 3, 0), (6, 0, 0),
-    (5, 1, 3, 0, 1), (5, 0, 4, 0, 1), (5, 0, 5, 0, 1), (5, 1, 2, 0, 0), (5, 0, 2, 0, 1), (5, 1, 4, 0, 0),
-    (5, 1, 5, 0, 0), (5, 1, 5, 0, 1), (5, 1, 4, 0, 1), (6, 0, 1), (6, 1, 0), (6, 1, 1),
+    (0, 1), (1, 1), (0, 0), (0, 3), (1, 0), (1, 3), (3, 4, 1), (2, 0), (3, 12, 0), (3, 4, 0), (3, 7, 1), (2, 1),
+    (3, 12, 1), (4, 0, 1), (3, 8, 1), (3, 7, 0), (3, 5, 1), (0, 2), (3, 8, 0), (3, 13, 1), (3, 1, 0),
+    (3, 15, 0), (3, 11, 1), (3, 15, 1), (3, 13, 0), (3, 5, 0), (1, 2), (4, 0, 5), (3, 3, 0), (2, 3), (3, 1, 1),
+    (4, 0, 4), (3, 9, 0), (4, 0, 0), (3, 11, 0), (3, 9, 1), (3, 3, 1), (3, 6, 0), (3, 14, 1), (4, 0, 7),
+    (3, 14, 0), (2, 2), (3, 6, 1), (3, 4, 3), (4, 0, 2), (3, 2, 1), (3, 12, 2), (3, 1, 3), (3, 2, 0), (4, 0, 3),
+    (3, 10, 0), (4, 0, 6), (3, 4, 2), (3, 10, 1), (3, 12, 3), (4, 0, 8), (5, 0, 0, 3, 0), (3, 3, 2), (4, 1, 0),
+    (5, 0, 0, 0, 0), (5, 0, 0, 1, 1), (3, 7, 3), (5, 0, 0, 2, 0), (3, 1, 2), (3, 15, 2), (4, 1, 1), (3, 3, 3),
+    (3, 5, 3), (3, 7, 2), (3, 15, 3), (3, 8, 2), (4, 1, 2), (5, 0, 0, 1, 0), (5, 0, 0, 3, 1), (3, 13, 2),
+    (5, 0, 0, 2, 1), (3, 8, 3), (3, 2, 2), (3, 2, 3), (3, 5, 2), (4, 1, 4), (3, 13, 3), (4, 1, 3), (4, 1, 5),
+    (3, 11, 2), (5, 0, 1, 0, 1), (3, 6, 2), (5, 0, 1, 3, 0), (5, 0, 2, 1, 1), (5, 0, 0, 0, 1), (5, 0, 2, 2, 0),
+    (5, 0, 2, 2, 1), (5, 0, 1, 2, 0), (3, 9, 2), (3, 14, 2), (5, 0, 2, 3, 1), (3, 11, 3), (5, 0, 1, 1, 0),
+    (3, 9, 3), (5, 0, 1, 1, 1), (4, 1, 7), (3, 10, 2), (5, 0, 2, 0, 0), (5, 0, 1, 0, 0), (3, 14, 3),
+    (5, 0, 2, 3, 0), (3, 6, 3), (4, 1, 6), (3, 10, 3), (5, 0, 1, 3, 1), (5, 0, 1, 2, 1), (4, 1, 8),
+    (5, 1, 0, 0, 0), (5, 1, 0, 2, 1), (5, 1, 0, 1, 1), (5, 1, 0, 2, 0), (5, 1, 0, 0, 1), (5, 1, 0, 3, 0),
+    (5, 1, 1, 1, 0), (5, 1, 1, 1, 1), (5, 1, 0, 3, 1), (5, 0, 3, 0, 1), (5, 1, 1, 0, 1), (5, 0, 2, 1, 0),
+    (5, 1, 0, 1, 0), (5, 1, 1, 2, 0), (5, 1, 2, 2, 0), (5, 1, 2, 1, 1), (5, 1, 2, 0, 0), (5, 1, 2, 2, 1),
+    (5, 1, 1, 2, 1), (5, 1, 2, 3, 1), (5, 1, 1, 3, 1), (5, 1, 1, 0, 0), (5, 0, 5, 0, 1), (5, 1, 2, 1, 0),
+    (5, 0, 3, 0, 0), (5, 1, 3, 0, 0), (5, 1, 1, 3, 0), (5, 1, 2, 3, 0), (5, 0, 4, 0, 0), (5, 1, 3, 0, 1),
+    (5, 1, 4, 0, 1), (5, 0, 2, 0, 1), (5, 0, 4, 0, 1), (5, 1, 4, 0, 0), (5, 1, 2, 0, 1), (5, 0, 5, 0, 0),
+    (5, 1, 5, 0, 0), (5, 1, 5, 0, 1), (6, 0, 0), (6, 0, 1), (6, 1, 0), (6, 1, 1),
 )
 
 
@@ -73,6 +74,7 @@
         copy.start()
 
     def partner(k):
+        k = lax.rem(k * STRIDE, SRC)
         r = lax.rem(row + lax.div(k, N_COL), N_ROW)
         a = lax.rem(cx + lax.rem(lax.div(k, RING), RING), RING)
         b = lax.rem(cy + lax.rem(k, RING), RING)
@@ -80,11 +82,20 @@
 
     barrier = pltpu.get_barrier_semaphore()
 
-    def greet(k, carry):
+    def each_partner(act):
+        def block(i, carry):
+            for j in range(8):
+                act(i * 8 + j + 1)
+            return carry
+
+        lax.fori_loop(0, SRC // 8 - 1, block, 0)
+        for j in range(SRC - 7, SRC):
+            act(jnp.int32(j))
+
+    def greet(k):
         pl.semaphore_signal(barrier, inc=1, device_id=partner(k), device_id_type=MESH)
-        return carry
-
-    lax.fori_loop(1, SRC, greet, 0)
+
+    each_partner(greet)
 
     for copy in inputs:
         copy.wait()
@@ -117,7 +128,7 @@
         outgoing[:, c] = picked.astype(BF16).reshape(N_ROW, CAP, WIDTH)
     pl.semaphore_wait(barrier, SRC - 1)
 
-    def spread(k, carry):
+    def spread(k):
         r, c = partner(k)
         pltpu.make_async_remote_copy(
             src_ref=outgoing.at[r, c],
@@ -127,9 +138,8 @@
             device_id=(r, c),
             device_id_type=MESH,
         ).start()
-        return carry
-
-    lax.fori_loop(1, SRC, spread, 0)
+
+    each_partner(spread)
     own_copy = pltpu.make_async_copy(outgoing.at[row, col], arrived.at[me], own_sem)
     own_copy.start()
 

time: 126 us -> 120 us (0.952); the launches traced: 124 us -> 120 us
  Pallas kernels: 122 us -> 118 us
    pallas_call x1, Pallas kernels: 122 us -> 118 us  [per_device(): pl.pallas_call(layer_kernel, out_shape=jax.ShapeDtypeStruct((TOK, WIDTH),...]
where the time goes in v1:
time: 120 us
  Pallas kernels  118 us (98%)
  local copies, waits for them, and re-layouts  1.87 us (2%)
    pallas_call x1, Pallas kernels, per_device(): pl.pallas_call(layer_kernel, out_shape=jax.ShapeDtypeStruct((TOK, WIDTH),...  118 us

profile of v1, /device:TPU:1, one launch (start us, length us, event | category | flops | bytes accessed | tf_op | source)
XLA Modules:
  0.0 120.0 jit_solution(16906295688237873577)
XLA Ops:
  0.0 118.2 %layer.1 = bf16[1024,256]{1,0:T(8,128)(2,1)} custom-call(s32[8,128]{1,0:T(8,128)} %bitcast.6, s32[8,128]{1,0:T(8,128)} %bitcast.7, bf16[64,4096]{1,0:T(8,128)(2,1)} %loaded_hbm.1, bf16[924,4096]{1,0:T(8,128)(2,1)} %bitcast.4, bf16[924,4096]{1,0:T(8,128)(2,1)} %bitcast.5, bf16[924,4096]{1,0:T(8,128)(2,1)} %wd_hbm.1), custom_call_target="tpu_custom_call" | custom-call | tf_op jit(solution)/shard_map/layer/pallas_call | solution.py:399
  118.2 1.9 %copy.8 = bf16[1024,256]{1,0:T(8,128)(2,1)} copy(bf16[1024,256]{1,0:T(8,128)(2,1)} %layer.1) | data formatting | bytes 1048576

commit v2 on v1

--- a/solution.py
+++ b/solution.py
@@ -50,8 +50,8 @@
 
 
 def layer_kernel(
-    len_hbm, off_hbm, loaded_hbm, wg_hbm, wu_hbm, wd_hbm, out,
-    len_t, off_t, loaded, outgoing, arrived, table, hot, w_in, wd, x, acc, hid, term, got,
+    len_t, off_t, loaded_hbm, wg_hbm, wu_hbm, wd_hbm, out,
+    loaded, outgoing, arrived, table, hot, w_in, wd, x, acc, hid, term, got,
     in_sem, w_sem, own_sem, spread_send, spread_recv, ag_send, ag_recv, rs_send, rs_recv,
 ):
     row = lax.axis_index("row")
@@ -63,7 +63,7 @@
     inputs = [
         pltpu.make_async_copy(src, dst, in_sem.at[i])
         for i, (src, dst) in enumerate(
-            ((len_hbm, len_t), (off_hbm, off_t), (loaded_hbm, loaded))
+            ((loaded_hbm, loaded),)
         )
     ]
     loads = [
@@ -395,15 +395,14 @@
 
 def per_device(loaded, lengths, offsets, gate_weight, up_weight, down_weight):
     width, hidden = gate_weight.shape
-    hbm = pl.BlockSpec(memory_space=pl.ANY)
+    hbm = pl.BlockSpec(memory_space=pltpu.HBM)
+    vmem = pl.BlockSpec(memory_space=pltpu.VMEM)
     return pl.pallas_call(
         layer_kernel,
         out_shape=jax.ShapeDtypeStruct((TOK, WIDTH), BF16),
-        in_specs=[hbm] * 6,
+        in_specs=[vmem] * 2 + [hbm] * 4,
         out_specs=pl.BlockSpec(memory_space=pltpu.VMEM),
         scratch_shapes=[
-            pltpu.VMEM((TRAJ, SRC), I32),
-            pltpu.VMEM((TRAJ, SRC), I32),
             pltpu.VMEM((LOAD, width), BF16),
             pltpu.VMEM((N_ROW, N_COL, CAP, WIDTH), BF16),
             pltpu.VMEM((SRC, CAP, WIDTH), BF16),
@@ -416,7 +415,7 @@
             pltpu.VMEM((TOK, hidden), BF16),
             pltpu.VMEM((PIECE, WIDTH), F32),
             pltpu.VMEM((60, PIECE, WIDTH), BF16),
-            pltpu.SemaphoreType.DMA((3,)),
+            pltpu.SemaphoreType.DMA((1,)),
             pltpu.SemaphoreType.DMA((3,)),
             pltpu.SemaphoreType.DMA,
             pltpu.SemaphoreType.DMA,
@@ -427,7 +426,7 @@
             pltpu.SemaphoreType.DMA((60,)),
         ],
         compiler_params=pltpu.CompilerParams(
-            collective_id=0, has_side_effects=True, vmem_limit_bytes=60 * 1024 * 1024
+            collective_id=0, has_side_effects=True, vmem_limit_bytes=53 * 1024 * 1024
         ),
         name="layer",
     )(lengths.T, offsets.T, loaded, gate_weight.T, up_weight.T, down_weight)

time: 120 us -> 120 us (level)
  no operation moved by 1% of the time
where the time goes in v2:
time: 120 us; the launch traced here: 119 us
  Pallas kernels  117 us (98%)
  local copies, waits for them, and re-layouts  2.17 us (2%)
    pallas_call x1, Pallas kernels, per_device(): pl.pallas_call(layer_kernel, out_shape=jax.ShapeDtypeStruct((TOK, WIDTH),...  117 us

profile of v2, /device:TPU:1, one launch (start us, length us, event | category | flops | bytes accessed | tf_op | source)
XLA Modules:
  0.0 119.4 jit_solution(11260025630667257486)
XLA Ops:
  0.0 0.0 copy-start
  0.0 0.7 copy-done
  0.7 0.0 copy-start.1
  0.7 0.7 copy-done.1
  1.4 117.3 %layer.1 = bf16[1024,256]{1,0:T(8,128)(2,1)S(1)} custom-call(s32[8,128]{1,0:T(8,128)S(1)} %bitcast.4, s32[8,128]{1,0:T(8,128)S(1)} %bitcast.5, bf16[64,4096]{1,0:T(8,128)(2,1)} %loaded_hbm.1, bf16[924,4096]{1,0:T(8,128)(2,1)} %bitcast.6, bf16[924,4096]{1,0:T(8,128)(2,1)} %bitcast.7, bf16[924,4096]{1,0:T(8,128)(2,1)} %wd_hbm.1), custom_call_target="tpu_custom_call" | custom-call | tf_op jit(solution)/shard_map/layer/pallas_call | solution.py:400
  118.6 0.8 copy.8
Async XLA Ops:
  0.0 0.7 copy-start
  0.7 0.7 copy-start.1
